TPU v7x, 256 devices: a whole 4x4x8 slice. The times are simulated.
256 devices in a mesh: grid: 64 (over z, y, core), orb: 4 (over x).
Axes of the slice: x: 4, y: 4, z: 8, core: 2. Of those that a mesh axis runs over, the one named last changes fastest.
Arguments:
- c_old: float32 [1024, 65536], P('orb', 'grid'), may hold values from -7 to 7
- c_trial: float32 [1024, 65536], P('orb', 'grid'), may hold values from -7 to 7
Outputs:
- c_new: float32 [1024, 65536], P('orb', 'grid')
- multiplier: float32 [1024, 1024], P('grid', 'orb')
All inputs are finite; a program needn't handle non-finite values.
Results may differ from a plain program's by a relative error of at most 0.0001.
Values sent between devices are 32-bit elements; how exact they have to be, the bound alone decides.
No kernel may reach another device: no remote copies, remote signals or barrier semaphores. Data moves between devices by JAX's collectives and lax.ppermute only.
A program may use at most 64 MiB of HBM per device.

v0:
```python
import jax
import jax.numpy as jnp
from jax import lax
from jax.sharding import PartitionSpec as P

ITERS = 4


def product(left, right):
    return jnp.dot(left, right, precision=lax.Precision.HIGHEST, preferred_element_type=jnp.float32)


def against(left, right):
    return lax.dot_general(
        left,
        right,
        (((1,), (1,)), ((), ())),
        precision=lax.Precision.HIGHEST,
        preferred_element_type=jnp.float32,
    )


def column_block(matrix):
    return lax.all_gather(matrix, "grid", axis=0, tiled=True)


def local(c_old, c_trial):
    grid_count = lax.axis_size("grid")
    orb_count = lax.axis_size("orb")
    block_orbs = c_old.shape[0]
    total_orbs = block_orbs * orb_count
    tile_rows = total_orbs // grid_count
    inverse = 1.0 / (c_old.shape[1] * grid_count)
    old_all, trial_all = (
        lax.all_gather(c_old, "orb", axis=0, tiled=True),
        lax.all_gather(c_trial, "orb", axis=0, tiled=True),
    )
    row_first = lax.axis_index("grid") * tile_rows
    pieces = (
        against(trial_all, c_trial),
        against(trial_all, c_old),
        against(old_all, c_trial),
        against(old_all, c_old),
    )
    stacked = lax.psum_scatter(
        jnp.concatenate(pieces, axis=1) * inverse, "grid", scatter_dimension=0, tiled=True
    )
    b_columns = lax.all_gather(
        stacked[:, 2 * block_orbs : 3 * block_orbs], "grid", axis=0, tiled=True
    )
    a_tile = stacked[:, :block_orbs]
    e_tile = stacked[:, block_orbs : 2 * block_orbs]
    s_tile = stacked[:, 3 * block_orbs :]
    e_rows, s_rows = (
        lax.all_gather(e_tile, "orb", axis=1, tiled=True),
        lax.all_gather(s_tile, "orb", axis=1, tiled=True),
    )
    row_numbers = row_first + lax.iota(jnp.int32, tile_rows)
    col_numbers = lax.axis_index("orb") * block_orbs + lax.iota(jnp.int32, block_orbs)
    identity = (row_numbers[:, None] == col_numbers[None, :]).astype(jnp.float32)
    multiplier = 0.5 * (identity - a_tile)
    for sweep in range(ITERS - 1):
        x_columns = column_block(multiplier)
        x_rows = lax.all_gather(multiplier, "orb", axis=1, tiled=True)
        y_columns = lax.all_gather(product(s_rows, x_columns), "grid", axis=0, tiled=True)
        multiplier = 0.5 * (
            identity
            - a_tile
            + 2.0 * multiplier
            - product(x_rows, b_columns)
            - product(e_rows, x_columns)
            - product(x_rows, y_columns)
        )
    x_columns = column_block(multiplier)
    moved = lax.dot_general(
        x_columns,
        old_all,
        (((0,), (0,)), ((), ())),
        precision=lax.Precision.HIGHEST,
        preferred_element_type=jnp.float32,
    )
    return (c_trial + moved, multiplier)


def solution(mesh):
    placed = (P("orb", "grid"), P("orb", "grid"))
    return jax.shard_map(
        local,
        mesh=mesh,
        in_specs=placed,
        out_specs=(P("orb", "grid"), P("grid", "orb")),
        check_vma=False,
    )
```

profile of v0, /device:TPU:1, one launch (start us, length us, event | category | flops | bytes accessed | tf_op | source)
XLA Modules:
  0.0 919.1 jit_solution(7348002993950733623)
XLA Ops:
  7.2 0.7 all-gather.13.cloned.1.call-update
  7.9 0.7 all-gather.11.cloned.1.call-update
  8.7 55.7 %all-gather.13.cloned.1.call-done = f32[1024,1024]{1,0:T(8,128)} async-done(((f32[256,1024]{1,0:T(8,128)}), f32[1024,1024]{1,0:T(8,128)}) %all-gather.13.cloned.1.call-update) | async-done | bytes 4194320 | tf_op jit(solution)/shard_map/all_gather | solution.py:35
  64.4 6.1 fusion.7
  70.6 4.9 fusion.8
  75.5 42.0 %all-gather.11.cloned.1.call-done = f32[1024,1024]{1,0:T(8,128)} async-done(((f32[256,1024]{1,0:T(8,128)}), f32[1024,1024]{1,0:T(8,128)}) %all-gather.11.cloned.1.call-update) | async-done | bytes 4194320 | tf_op jit(solution)/shard_map/all_gather | solution.py:36
  117.5 6.2 fusion.5
  123.7 3.9 fusion.6
  127.6 2.7 maximum_multiply_fusion
  130.3 5.4 copy.16
  135.8 0.0 all-gather.17.cloned.1.call-start
  135.8 139.2 %reduce-scatter.4.cloned.1.call-done = f32[16,1024]{1,0:T(8,128)} async-done(((f32[1024,1024]{1,0:T(8,128)}), f32[16,1024]{1,0:T(8,128)}) %reduce-scatter.4.cloned.1.call-update) | async-done | bytes 65552 | tf_op jit(solution)/shard_map/reduce_scatter | solution.py:45
  275.1 1.4 fusion.4
  276.5 0.0 all-gather.15.cloned.1.call-start
  276.6 0.5 all-gather.15.cloned.1.call-update
  277.2 0.1 copy.20
  277.3 10.2 %all_gather.51 = f32[16,1024]{0,1:T(8,128)S(1)} all-gather(f32[16,256]{0,1:T(8,128)S(1)} %copy.20), channel_id=1, replica_groups=mesh['grid'=64,'orb'=4] {'orb'}, dimensions={1}, use_global_device_ids=true | all-gather | bytes 81920 | tf_op jit(solution)/shard_map/all_gather | solution.py:56
  287.5 71.5 %all-gather.17.cloned.1.call-done = f32[1024,256]{1,0:T(8,128)} async-done(((f32[16,256]{1,0:T(8,128)}), f32[1024,256]{1,0:T(8,128)}) %all-gather.17.cloned.1.call-update) | async-done | bytes 1048592 | tf_op jit(solution)/shard_map/all_gather | solution.py:24
  358.9 2.8 fusion.9
  361.7 0.0 all-gather.21.cloned.1.call-start
  361.8 0.1 copy.19
  361.9 9.8 %all_gather.47 = f32[16,1024]{1,0:T(8,128)S(1)} all-gather(f32[16,256]{1,0:T(8,128)} %get-tuple-element.5), channel_id=1, replica_groups=mesh['grid'=64,'orb'=4] {'orb'}, dimensions={1}, use_global_device_ids=true | all-gather | bytes 81920 | tf_op jit(solution)/shard_map/all_gather | solution.py:64
  371.7 10.6 %all_gather.49 = f32[16,1024]{0,1:T(8,128)S(1)} all-gather(f32[16,256]{0,1:T(8,128)S(1)} %copy.19), channel_id=1, replica_groups=mesh['grid'=64,'orb'=4] {'orb'}, dimensions={1}, use_global_device_ids=true | all-gather | bytes 81920 | tf_op jit(solution)/shard_map/all_gather | solution.py:55
  382.3 54.2 %all-gather.15.cloned.1.call-done = f32[1024,256]{1,0:T(8,128)} async-done(((f32[16,256]{1,0:T(8,128)}), f32[1024,256]{1,0:T(8,128)}) %all-gather.15.cloned.1.call-update) | async-done | bytes 1048592 | tf_op jit(solution)/shard_map/all_gather | solution.py:48
  436.6 1.8 convolution_subtract_fusion.5
  438.4 75.3 %all-gather.19.cloned.1.call-done = f32[1024,256]{1,0:T(8,128)} async-done(((f32[16,256]{1,0:T(8,128)}), f32[1024,256]{1,0:T(8,128)}) %all-gather.19.cloned.1.call-update) | async-done | bytes 1048592 | tf_op jit(solution)/shard_map/all_gather | solution.py:65
  513.7 1.7 fusion.10
  515.4 2.8 broadcast_multiply_fusion.1
  518.2 0.0 all-gather.23.cloned.1.call-start
  518.3 74.2 %all-gather.21.cloned.1.call-done = f32[1024,256]{1,0:T(8,128)} async-done(((f32[16,256]{1,0:T(8,128)}), f32[1024,256]{1,0:T(8,128)}) %all-gather.21.cloned.1.call-update) | async-done | bytes 1048592 | tf_op jit(solution)/shard_map/all_gather | solution.py:24
  592.5 2.8 fusion.11
  595.3 0.0 all-gather.25.cloned.1.call-start
  595.3 9.8 %all_gather.53 = f32[16,1024]{1,0:T(8,128)S(1)} all-gather(f32[16,256]{1,0:T(8,128)} %get-tuple-element.8), channel_id=1, replica_groups=mesh['grid'=64,'orb'=4] {'orb'}, dimensions={1}, use_global_device_ids=true | all-gather | bytes 81920 | tf_op jit(solution)/shard_map/all_gather | solution.py:64
  605.2 0.5 convolution_subtract_fusion.4
  605.7 64.6 %all-gather.23.cloned.1.call-done = f32[1024,256]{1,0:T(8,128)} async-done(((f32[16,256]{1,0:T(8,128)}), f32[1024,256]{1,0:T(8,128)}) %all-gather.23.cloned.1.call-update) | async-done | bytes 1048592 | tf_op jit(solution)/shard_map/all_gather | solution.py:65
  670.3 1.7 fusion.12
  672.0 2.8 broadcast_multiply_fusion
  674.9 0.0 all-gather.27.cloned.1.call-start
  674.9 74.2 %all-gather.25.cloned.1.call-done = f32[1024,256]{1,0:T(8,128)} async-done(((f32[16,256]{1,0:T(8,128)}), f32[1024,256]{1,0:T(8,128)}) %all-gather.25.cloned.1.call-update) | async-done | bytes 1048592 | tf_op jit(solution)/shard_map/all_gather | solution.py:24
  749.1 2.8 fusion.13
  751.9 0.0 all-gather.29.cloned.1.call-start
  751.9 10.1 %all_gather.56 = f32[16,1024]{1,0:T(8,128)S(1)} all-gather(f32[16,256]{1,0:T(8,128)} %get-tuple-element.10), channel_id=1, replica_groups=mesh['grid'=64,'orb'=4] {'orb'}, dimensions={1}, use_global_device_ids=true | all-gather | bytes 81920 | tf_op jit(solution)/shard_map/all_gather | solution.py:64
  762.0 0.5 convolution_subtract_fusion.3
  762.5 64.2 %all-gather.27.cloned.1.call-done = f32[1024,256]{1,0:T(8,128)} async-done(((f32[16,256]{1,0:T(8,128)}), f32[1024,256]{1,0:T(8,128)}) %all-gather.27.cloned.1.call-update) | async-done | bytes 1048592 | tf_op jit(solution)/shard_map/all_gather | solution.py:65
  826.7 1.7 fusion.14
  828.5 2.8 fusion.3
  831.3 74.2 %all-gather.29.cloned.1.call-done = f32[1024,256]{1,0:T(8,128)} async-done(((f32[16,256]{1,0:T(8,128)}), f32[1024,256]{1,0:T(8,128)}) %all-gather.29.cloned.1.call-update) | async-done | bytes 1048592 | tf_op jit(solution)/shard_map/all_gather | solution.py:24
  905.5 7.1 convolution_add_fusion
  (28 shorter events, 0.3 us)
Async XLA Ops:
  7.2 57.3 %all-gather.13.cloned.1.call-start = ((), (), s32[]{:S(2)}) async-start(), calls=%async_computation.2 | async-start | bytes 5242880 | tf_op jit(solution)/shard_map/all_gather | solution.py:35
  7.2 63.4 %copy-start.4 = (f32[256,1024]{1,0:T(8,128)S(1)}, f32[256,1024]{1,0:T(8,128)}, u32[]{:S(2)}) copy-start(f32[256,1024]{1,0:T(8,128)} %param.2) | copy-start | bytes 3145732
  7.9 109.6 %all-gather.11.cloned.1.call-start = ((), (), s32[]{:S(2)}) async-start(), calls=%async_computation.1 | async-start | bytes 5242880 | tf_op jit(solution)/shard_map/all_gather | solution.py:36
  8.6 266.4 %reduce-scatter.4.cloned.1.call-start = ((), (), s32[]{:S(2)}) async-start(), calls=%async_computation.11 | async-start | bytes 4259840 | tf_op jit(solution)/shard_map/reduce_scatter | solution.py:45
  64.4 6.2 copy-start
  70.6 46.8 %copy-start.2 = (f32[256,1024]{1,0:T(8,128)S(1)}, f32[256,1024]{1,0:T(8,128)}, u32[]{:S(2)}) copy-start(f32[256,1024]{1,0:T(8,128)} %param.3) | copy-start | bytes 3145732
  117.5 6.2 copy-start.1
  123.7 3.9 copy-start.5
  135.8 223.1 %all-gather.17.cloned.1.call-start = ((), (), s32[]{:S(2)}) async-start(), calls=%async_computation.4 | async-start | bytes 1064960 | tf_op jit(solution)/shard_map/all_gather | solution.py:24
  276.5 160.0 %all-gather.15.cloned.1.call-start = ((), (), s32[]{:S(2)}) async-start(), calls=%async_computation.3 | async-start | bytes 1064960 | tf_op jit(solution)/shard_map/all_gather | solution.py:48
  277.1 236.6 %all-gather.19.cloned.1.call-start = ((), (), s32[]{:S(2)}) async-start(), calls=%async_computation.5 | async-start | bytes 1064960 | tf_op jit(solution)/shard_map/all_gather | solution.py:65
  287.4 317.7 %copy-start.6 = (f32[16,1024]{1,0:T(8,128)S(1)}, f32[16,1024]{1,0:T(8,128)}, u32[]{:S(2)}) copy-start(f32[16,1024]{1,0:T(8,128)} %reduce-scatter.4.cloned.1.call-done) | copy-start | bytes 196612
  361.7 230.8 %all-gather.21.cloned.1.call-start = ((), (), s32[]{:S(2)}) async-start(), calls=%async_computation.6 | async-start | bytes 1064960 | tf_op jit(solution)/shard_map/all_gather | solution.py:24
  436.6 168.6 %copy-start.3 = (f32[1024,256]{1,0:T(8,128)S(1)}, f32[1024,256]{1,0:T(8,128)}, u32[]{:S(2)}) copy-start(f32[1024,256]{1,0:T(8,128)} %all-gather.15.cloned.1.call-done) | copy-start | bytes 3145732
  518.2 152.0 %all-gather.23.cloned.1.call-start = ((), (), s32[]{:S(2)}) async-start(), calls=%async_computation.7 | async-start | bytes 1064960 | tf_op jit(solution)/shard_map/all_gather | solution.py:65
  595.3 153.8 %all-gather.25.cloned.1.call-start = ((), (), s32[]{:S(2)}) async-start(), calls=%async_computation.8 | async-start | bytes 1064960 | tf_op jit(solution)/shard_map/all_gather | solution.py:24
  674.9 151.9 %all-gather.27.cloned.1.call-start = ((), (), s32[]{:S(2)}) async-start(), calls=%async_computation.9 | async-start | bytes 1064960 | tf_op jit(solution)/shard_map/all_gather | solution.py:65
  751.9 153.6 %all-gather.29.cloned.1.call-start = ((), (), s32[]{:S(2)}) async-start(), calls=%async_computation.10 | async-start | bytes 1064960 | tf_op jit(solution)/shard_map/all_gather | solution.py:24
Sparse Core Ops, SparseCore 0:
  9.8 54.5 all-gather.12
  66.2 51.1 all-gather.10
  135.9 139.1 reduce-scatter.3
  278.6 80.2 all-gather.16
  362.5 74.0 all-gather.14
  439.6 74.0 all-gather.18
  518.4 74.0 all-gather.20
  596.2 74.0 all-gather.22
  675.0 74.0 all-gather.24
  752.6 74.0 all-gather.26
  831.4 74.0 all-gather.28
where the time goes:
time: 920 us; the launch traced here: 919 us
  waiting for transfers between devices  791 us (86%)
  matrix products  53 us (6%)
  blocking collectives  50.6 us (6%)
  between operations  14 us (2%)
    all_gather x4, waiting for transfers between devices, column_block(): return lax.all_gather(matrix, 'grid', axis=0, tiled=True)  294 us
    all_gather x3, waiting for transfers between devices, local(): lax.all_gather(product(s_rows, x_columns), 'grid', axis=0, tiled=True)  204 us
    reduce_scatter x1, waiting for transfers between devices, local(): lax.psum_scatter(jnp.concatenate(pieces, axis=1) * inverse, 'grid', scatt...  139 us
    all_gather x1, waiting for transfers between devices, local(): lax.all_gather(c_old, 'orb', axis=0, tiled=True)  55.7 us
    all_gather x1, waiting for transfers between devices, local(): lax.all_gather(stacked[:, 2 * block_orbs:3 * block_orbs], 'grid', axis=0,...  54.2 us
    all_gather x1, waiting for transfers between devices, local(): lax.all_gather(c_trial, 'orb', axis=0, tiled=True)  42 us
    all_gather x3, blocking collectives, local(): x_rows = lax.all_gather(multiplier, 'orb', axis=1, tiled=True)  29.8 us
    dot_general x12, matrix products, product(): jnp.dot(left, right, precision=lax.Precision.HIGHEST, preferred_element_t...  24.9 us
  transfers between devices with their start and end apart: 11, of which 11 were waited for; matrix products, arithmetic and copies ran while one was open for 2% of the time, Pallas kernels for 0%

commit v1 on v0

v1 whole, which is shorter than its diff:
```python
import jax
import jax.numpy as jnp
from jax import lax
from jax.sharding import Mesh, PartitionSpec as P

ITERS = 4
NX, NY, NZ, NC = 4, 4, 8, 2
HIGH = lax.Precision.HIGH


def product(left, right, dims=((1,), (0,))):
    return lax.dot_general(
        left, right, (dims, ((), ())), precision=HIGH, preferred_element_type=jnp.float32
    )


def from_offset(value, axis, size, offset):
    return lax.ppermute(value, axis, [((i + offset) % size, i) for i in range(size)])


def ring_gather(value, axis, size):
    return [value] + [from_offset(value, axis, size, r) for r in range(1, size)]


def to_tiles(matrix):
    rows, cols = matrix.shape
    return (
        matrix.reshape(rows // 8, 8, cols // 128, 128)
        .transpose(0, 2, 1, 3)
        .reshape(rows * cols // 1024, 8, 128)
    )


def from_tiles(tiles, cols):
    rows = tiles.shape[0] * 1024 // cols
    return (
        tiles.reshape(rows // 8, cols // 128, 8, 128).transpose(0, 2, 1, 3).reshape(rows, cols)
    )


def reduce_over_grid(tiles):
    count = tiles.shape[0]
    core = lax.axis_index("core")
    half = count // NC
    keep = lax.dynamic_slice_in_dim(tiles, core * half, half, 0)
    send = lax.dynamic_slice_in_dim(tiles, (1 - core) * half, half, 0)
    tiles = keep + from_offset(send, "core", NC, 1)
    for axis, size in (("y", NY), ("z", NZ)):
        tiles = tiles.reshape((size, tiles.shape[0] // size) + tiles.shape[1:])
        tiles = jnp.sum(lax.all_to_all(tiles, axis, 0, 0), axis=0)
    return tiles


def gather_over_z(tiles):
    spread = jnp.broadcast_to(tiles[None], (NZ,) + tiles.shape)
    return lax.all_to_all(spread, "z", 0, 0).reshape((-1,) + tiles.shape[1:])


def gather_over_y(tiles):
    parts = ring_gather(tiles, "y", NY)
    place = lax.axis_index("y")
    stacked = jnp.stack(parts)
    ordered = jnp.concatenate([stacked, stacked])
    return lax.dynamic_slice_in_dim(ordered, (NY - place) % NY, NY, 0).reshape(
        (-1,) + tiles.shape[1:]
    )


def gather_over_core(tiles):
    other = from_offset(tiles, "core", NC, 1)
    first = lax.axis_index("core") == 0
    return jnp.concatenate(
        [jnp.where(first, tiles, other), jnp.where(first, other, tiles)], axis=0
    )


def local(c_old, c_trial):
    block, slab = c_old.shape
    total = block * NX
    inverse = 1.0 / (slab * NC * NY * NZ)
    old_parts = ring_gather(c_old, "x", NX)
    trial_parts = ring_gather(c_trial, "x", NX)
    both = jnp.concatenate([c_trial, c_old], axis=0)
    against = ((1,), (1,))
    es = jnp.concatenate([product(both, part, against) for part in old_parts], axis=1)
    a = jnp.concatenate([product(c_trial, part, against) for part in trial_parts], axis=1)
    partial = jnp.concatenate([a, es], axis=0) * inverse
    mine = gather_over_y(gather_over_z(reduce_over_grid(to_tiles(partial))))
    blocks = []
    for offset, tiles in enumerate(ring_gather(mine, "x", NX)):
        rows = from_tiles(gather_over_core(tiles), total)
        blocks.append(jnp.roll(rows, offset * block, axis=1))
    a, e, s = (
        jnp.concatenate([rows[i * block : (i + 1) * block] for rows in blocks], axis=0)
        for i in range(3)
    )
    identity = jnp.eye(total, dtype=jnp.float32)
    start = identity - a
    x = 0.5 * start
    for sweep in range(ITERS - 2):
        q = product((identity - e) - 0.5 * product(x, s), x)
        x = 0.5 * (start + q + q.T)
    x_col, x_row = x[:, :block], x[:block]
    w_row = (identity - e)[:block] - 0.5 * product(x_row, s)
    q_row = product(w_row, x)
    q_col = x_col - product(e, x_col) - 0.5 * product(x, product(s, x_col))
    x_col = 0.5 * (start[:, :block] + q_col + q_row.T)
    old_all = jnp.concatenate(old_parts, axis=0)
    c_new = c_trial + product(x_col, old_all, ((0,), (0,)))
    grid_place = (lax.axis_index("z") * NY + lax.axis_index("y")) * NC + lax.axis_index("core")
    tile_rows = total // (NZ * NY * NC)
    first = (grid_place * tile_rows - lax.axis_index("x") * block) % total
    return c_new, lax.dynamic_slice_in_dim(x_col, first, tile_rows, 0)


def solution(mesh):
    fine = Mesh(mesh.devices.reshape(NZ, NY, NC, NX), ("z", "y", "core", "x"))
    grid = ("z", "y", "core")
    return jax.shard_map(
        local,
        mesh=fine,
        in_specs=(P("x", grid), P("x", grid)),
        out_specs=(P("x", grid), P(grid, "x")),
        check_vma=False,
    )
```

time: 920 us -> 374 us (0.41)
  waiting for transfers between devices: 791 us -> 132 us
  starting transfers between devices: 0.45 us -> 55.5 us
  matrix products: 53 us -> 73.2 us
  local copies, waits for them, and re-layouts: 5.68 us -> 25.8 us
  other arithmetic: 4.19 us -> 22 us
  between operations: 14 us -> 1.45 us
    all_gather x10 -> x0, waiting for transfers between devices: 650 us -> none  [the longest x4 294 us: column_block(): return lax.all_gather(matrix, 'grid', axis=0, tiled=True)]
    reduce_scatter x1 -> x0, waiting for transfers between devices: 139 us -> none  [local(): lax.psum_scatter(jnp.concatenate(pieces, axis=1) * inverse, 'grid', scatt...]
    ppermute x0 -> x17, waiting for transfers between devices: none -> 132 us  [from_offset(): lax.ppermute(value, axis, [((i + offset) % size, i) for i in range(size)])]
    all_to_all x0 -> x3, blocking collectives: none -> 58.8 us  [the longest x2 43.5 us: reduce_over_grid(): tiles = jnp.sum(lax.all_to_all(tiles, axis, 0, 0), axis=0)]
    ppermute x0 -> x17, starting transfers between devices: none -> 55.5 us  [from_offset(): lax.ppermute(value, axis, [((i + offset) % size, i) for i in range(size)])]
    all_gather x5 -> x0, blocking collectives: 50.6 us -> none  [the longest x3 29.8 us: local(): x_rows = lax.all_gather(multiplier, 'orb', axis=1, tiled=True)]
    dot_general x17 -> x18, matrix products: 53 us -> 73.2 us  [product(): lax.dot_general(left, right, (dims, ((), ())), precision=HIGH, preferred_...]
    dot_general x0 -> x2, local copies, waits for them, and re-layouts: none -> 10.9 us  [product(): lax.dot_general(left, right, (dims, ((), ())), precision=HIGH, preferred_...]
  transfers between devices with their start and end apart: 11 -> 17, of which waited for: 11 -> 9; matrix products, arithmetic and copies ran while one was open for 2% -> 6% of each run, Pallas kernels for 0% -> 0%
where the time goes in v1:
time: 374 us; the launch traced here: 369 us
  waiting for transfers between devices  132 us (35%)
  matrix products  73.2 us (20%)
  blocking collectives  58.8 us (16%)
  starting transfers between devices  55.5 us (15%)
  local copies, waits for them, and re-layouts  25.8 us (7%)
  other arithmetic  22 us (6%)
    ppermute x17, waiting for transfers between devices, from_offset(): lax.ppermute(value, axis, [((i + offset) % size, i) for i in range(size)])  132 us
    dot_general x18, matrix products, product(): lax.dot_general(left, right, (dims, ((), ())), precision=HIGH, preferred_...  73.2 us
    ppermute x17, starting transfers between devices, from_offset(): lax.ppermute(value, axis, [((i + offset) % size, i) for i in range(size)])  55.5 us
    all_to_all x2, blocking collectives, reduce_over_grid(): tiles = jnp.sum(lax.all_to_all(tiles, axis, 0, 0), axis=0)  43.5 us
    all_to_all x1, blocking collectives, gather_over_z(): return lax.all_to_all(spread, 'z', 0, 0).reshape((-1,) + tiles.shape[1:])  15.3 us
    dot_general x2, local copies, waits for them, and re-layouts, product(): lax.dot_general(left, right, (dims, ((), ())), precision=HIGH, preferred_...  10.9 us
  transfers between devices with their start and end apart: 17, of which 9 were waited for; matrix products, arithmetic and copies ran while one was open for 6% of the time, Pallas kernels for 0%

profile of v1, /device:TPU:1, one launch (start us, length us, event | category | flops | bytes accessed | tf_op | source)
XLA Modules:
  0.0 368.8 jit_solution(16771265593862308191)
XLA Ops:
  0.6 2.1 collective-permute-start.2
  4.0 1.3 collective-permute-start.4
  5.3 2.0 collective-permute-start.3
  7.8 1.3 constant_dynamic-update-slice_fusion.1
  10.4 2.2 fusion.59
  13.3 11.6 %collective-permute-done.2 = f32[256,1024]{1,0:T(8,128)} collective-permute-done((f32[256,1024]{1,0:T(8,128)}, f32[256,1024]{1,0:T(8,128)}, u32[]{:S(2)}, u32[]{:S(2)}) %collective-permute-start.2) | collective-permute-done | bytes 1048608 | tf_op jit(solution)/shard_map/ppermute | solution.py:18
  24.9 3.7 collective-permute-start
  28.6 1.8 fusion.58
  30.4 65.1 %collective-permute-done.1 = f32[256,1024]{1,0:T(8,128)} collective-permute-done((f32[256,1024]{1,0:T(8,128)}, f32[256,1024]{1,0:T(8,128)}, u32[]{:S(2)}, u32[]{:S(2)}) %collective-permute-start.1) | collective-permute-done | bytes 1048608 | tf_op jit(solution)/shard_map/ppermute | solution.py:18
  95.5 1.8 fusion.57
  97.4 2.2 fusion.62
  99.6 2.2 fusion.61
  101.9 2.2 fusion.60
  104.8 3.8 %maximum_multiply_fusion = f32[768,1024]{0,1:T(8,128)} fusion(f32[512,256]{0,1:T(8,128)S(1)} %fusion.62, f32[512,256]{0,1:T(8,128)S(1)} %fusion.61, f32[512,256]{0,1:T(8,128)S(1)} %fusion.60, f32[512,256]{0,1:T(8,128)S(1)} %fusion.59, f32[256,256]{0,1:T(8,128)S(1)} %fusion.58, f32[256,256]{0,1:T(8,128)S(1)} %fusion.57, f32[256,256]{0,1:T(8,128)S(1)} %fusion.56, ...), kind=kLoop, calls=%fused_computation.51 | loop fusion | flops 6291456 | bytes 6291456 | tf_op jit(solution)/shard_map/mul | solution.py:87
  108.6 3.6 copy.27
  112.2 2.6 copy.33
  115.6 1.6 copy-done.5
  118.4 1.5 collective-permute-start.6
  120.0 3.2 collective-permute-done.6
  123.2 1.6 dynamic-slice_add_fusion
  124.8 23.8 %all_to_all.15 = f32[4,96,8,128]{3,2,1,0:T(8,128)S(1)} all-to-all(f32[4,96,8,128]{3,2,1,0:T(8,128)S(1)} %bitcast.98), channel_id=1, replica_groups=mesh['z'=8,'y'=4,'core'=2,'x'=4] {'y'}, dimensions={0} | all-to-all | bytes 3145728 | tf_op jit(solution)/shard_map/all_to_all | solution.py:50
  148.7 19.6 %all_to_all.16 = f32[8,12,8,128]{3,2,1,0:T(8,128)S(1)} all-to-all(f32[8,12,8,128]{3,2,1,0:T(8,128)S(1)} %bitcast.108), channel_id=1, replica_groups=mesh['z'=8,'y'=4,'core'=2,'x'=4] {'z'}, dimensions={0} | all-to-all | bytes 786432 | tf_op jit(solution)/shard_map/all_to_all | solution.py:50
  168.4 15.3 %all_to_all.17 = f32[8,12,8,128]{3,2,1,0:T(8,128)S(1)} all-to-all(f32[8,12,8,128]{3,2,1,0:T(8,128)S(1)} %broadcast_in_dim.2), channel_id=1, replica_groups=mesh['z'=8,'y'=4,'core'=2,'x'=4] {'z'}, dimensions={0} | all-to-all | bytes 786432 | tf_op jit(solution)/shard_map/all_to_all | solution.py:56
  186.3 4.1 %collective-permute-done.7 = f32[96,8,128]{2,1,0:T(8,128)S(1)} collective-permute-done((f32[96,8,128]{2,1,0:T(8,128)S(1)}, f32[96,8,128]{2,1,0:T(8,128)S(1)}, u32[]{:S(2)}, u32[]{:S(2)}) %collective-permute-start.7) | collective-permute-done | bytes 393248 | tf_op jit(solution)/shard_map/ppermute | solution.py:18
  190.4 2.5 collective-permute-done.8
  192.9 11.2 %collective-permute-done.9 = f32[96,8,128]{2,1,0:T(8,128)S(1)} collective-permute-done((f32[96,8,128]{2,1,0:T(8,128)S(1)}, f32[96,8,128]{2,1,0:T(8,128)S(1)}, u32[]{:S(2)}, u32[]{:S(2)}) %collective-permute-start.9) | collective-permute-done | bytes 393248 | tf_op jit(solution)/shard_map/ppermute | solution.py:18
  204.5 2.7 collective-permute-start.11
  207.1 2.6 collective-permute-start.10
  209.7 31.8 %collective-permute-done.15 = f32[384,8,128]{2,1,0:T(8,128)} collective-permute-done((f32[384,8,128]{2,1,0:T(8,128)S(1)}, f32[384,8,128]{2,1,0:T(8,128)}, u32[]{:S(2)}, u32[]{:S(2)}) %collective-permute-start.15) | collective-permute-done | bytes 1572896 | tf_op jit(solution)/shard_map/ppermute | solution.py:18
  241.5 34.8 %collective-permute-start.16 = (f32[384,8,128]{2,1,0:T(8,128)}, f32[384,8,128]{2,1,0:T(8,128)}, u32[]{:S(2)}, u32[]{:S(2)}) collective-permute-start(f32[384,8,128]{2,1,0:T(8,128)} %collective-permute-done.15), channel_id=1, source_target_pairs={{4,0},{0,4},{5,1},{1,5},{6,2},{2,6},{7,3},{3,7},{12,8},{8,12},{13,... | collective-permute-start | bytes 4718600 | tf_op jit(solution)/shard_map/ppermute | solution.py:18
  276.8 1.6 broadcast_select_fusion.7
  279.7 2.1 broadcast_select_fusion.1
  282.3 1.9 collective-permute-done.12
  284.2 2.1 broadcast_select_fusion.5
  286.8 1.6 broadcast_select_fusion.3
  290.9 7.1 %fusion.22 = f32[1024,1024]{1,0:T(8,128)S(1)} fusion(f32[1024,1024]{1,0:T(8,128)S(1)} %fusion, f32[256,1024]{1,0:T(8,128)S(1)} %get-tuple-element.15, f32[256,1024]{1,0:T(8,128)S(1)} %get-tuple-element.13, f32[256,1024]{1,0:T(8,128)S(1)} %get-tuple-element.28, f32[256,1024]{1,0:T(8,128)S(1)} %get-tuple-element.8), kind=kOutput, calls=%fused_computation.40 | convolution fusion | flops 6449790976 | bytes 12582912 | tf_op jit(solution)/shard_map/dot_general | solution.py:12
  298.1 9.0 %fusion.16 = f32[1024,1024]{1,0:T(8,128)} fusion(f32[1024,1024]{1,0:T(8,128)S(1)} %fusion.22, f32[256,1024]{1,0:T(8,128)S(1)} %get-tuple-element.16, f32[256,1024]{1,0:T(8,128)S(1)} %get-tuple-element.14, f32[256,1024]{1,0:T(8,128)S(1)} %get-tuple-element.27, f32[256,1024]{1,0:T(8,128)S(1)} %get-tuple-element.10, f32[256,1024]{1,0:T(8,128)S(1)} %get-tuple-element.15, ...), kind=kOutput, calls=%fused_computation.29 | convolution fusion | flops 6458179584 | bytes 16777216 | tf_op jit(solution)/shard_map/dot_general | solution.py:12
  307.1 5.3 %copy.29 = f32[1024,1024]{0,1:T(8,128)} copy(f32[1024,1024]{1,0:T(8,128)} %fusion.16) | data formatting | bytes 8388608 | tf_op jit(solution)/shard_map/dot_general | solution.py:12
  312.4 13.7 %fusion.52 = f32[1024,1024]{1,0:T(8,128)} fusion(f32[1024,1024]{1,0:T(8,128)} %copy-done, f32[1024,1024]{0,1:T(8,128)} %copy.29, f32[1024,1024]{1,0:T(8,128)} %fusion.16, f32[256,1024]{1,0:T(8,128)} %copy-done.8, f32[256,1024]{1,0:T(8,128)} %copy-done.6, f32[256,1024]{1,0:T(8,128)} %copy-done.10, f32[256,1024]{1,0:T(8,128)} %copy-done.11), kind=kOutput, calls=%fused_computation.109 | convolution fusion | flops 6451888128 | bytes 20971520 | tf_op jit(solution)/shard_map/dot_general | solution.py:12
  326.1 13.7 %fusion.13 = f32[1024,1024]{1,0:T(8,128)} fusion(f32[1024,1024]{1,0:T(8,128)} %fusion.52, f32[1024,1024]{0,1:T(8,128)S(1)} %copy-done.4, f32[1024,1024]{1,0:T(8,128)S(1)} %copy-done.3, f32[256,1024]{1,0:T(8,128)} %copy-done.15, f32[256,1024]{1,0:T(8,128)} %copy-done.13, f32[256,1024]{1,0:T(8,128)} %copy-done.17, f32[256,1024]{1,0:T(8,128)} %copy-done.19, ...), kind=kOutput, calls=%fused_computation.26 | convolution fusion | flops 6460276736 | bytes 25165824 | tf_op jit(solution)/shard_map/dot_general | solution.py:12
  339.8 5.5 %copy.30 = f32[1024,1024]{0,1:T(8,128)} copy(f32[1024,1024]{1,0:T(8,128)} %fusion.13) | data formatting | bytes 8388608 | tf_op jit(solution)/shard_map/dot_general | solution.py:12
  345.4 5.5 %convert_subtract_fusion.1 = (f32[1024,1024]{1,0:T(8,128)S(1)}, f32[1024,1024]{1,0:T(8,128)S(1)}) fusion(f32[256,1024]{1,0:T(8,128)S(1)} %copy-done.9, f32[256,1024]{1,0:T(8,128)S(1)} %copy-done.7, f32[256,1024]{1,0:T(8,128)} %copy-done.10, f32[256,1024]{1,0:T(8,128)} %copy-done.11, f32[1024,1024]{0,1:T(8,128)} %copy.30, f32[1024,1024]{1,0:T(8,128)} %fusion.13), kind=kLoop, calls=%fused_computation.5 | loop fusion | flops 9437184 | bytes 20971520 | tf_op jit(solution)/shard_map/sub | solution.py:98
  350.9 1.8 fusion.28
  353.1 1.8 fusion.44
  355.8 2.1 fusion.30
  357.9 1.9 fusion.32
  359.8 3.5 fusion.29
  363.9 4.8 %fusion.33 = f32[256,1024]{1,0:T(8,128)} fusion(f32[256,1024]{1,0:T(8,128)S(1)} %copy-done.2, f32[1024,256]{1,0:T(8,128)S(1)} %fusion.29, f32[256,1024]{1,0:T(8,128)} %collective-permute-done.5, f32[256,1024]{1,0:T(8,128)} %collective-permute-done.4, f32[256,1024]{1,0:T(8,128)} %collective-permute-done.3, f32[256,1024]{1,0:T(8,128)S(1)} %copy-done.12), kind=kOutput, calls=%fused_computation.69 | convolution fusion | flops 1614020608 | bytes 7340032 | tf_op jit(solution)/shard_map/dot_general | solution.py:12
  (91 shorter events, 16.4 us)
Async XLA Ops:
  0.6 12.1 %copy-start.2 = (f32[256,1024]{1,0:T(8,128)S(1)}, f32[256,1024]{1,0:T(8,128)}, u32[]{:S(2)}) copy-start(f32[256,1024]{1,0:T(8,128)} %param.3) | copy-start | bytes 3145732
  0.6 24.3 %collective-permute-start.2 = (f32[256,1024]{1,0:T(8,128)}, f32[256,1024]{1,0:T(8,128)}, u32[]{:S(2)}, u32[]{:S(2)}) collective-permute-start(f32[256,1024]{1,0:T(8,128)} %param.3), channel_id=1, source_target_pairs={{3,0},{0,1},{1,2},{2,3},{7,4},{4,5},{5,6},{6,7},{11,8},{8,9},{9,10... | collective-permute-start | bytes 3145736 | tf_op jit(solution)/shard_map/ppermute | solution.py:18
  2.8 94.6 %collective-permute-start.5 = (f32[256,1024]{1,0:T(8,128)}, f32[256,1024]{1,0:T(8,128)}, u32[]{:S(2)}, u32[]{:S(2)}) collective-permute-start(f32[256,1024]{1,0:T(8,128)} %param.2), channel_id=1, source_target_pairs={{3,0},{0,1},{1,2},{2,3},{7,4},{4,5},{5,6},{6,7},{11,8},{8,9},{9,10... | collective-permute-start | bytes 3145736 | tf_op jit(solution)/shard_map/ppermute | solution.py:18
  4.0 95.6 %collective-permute-start.4 = (f32[256,1024]{1,0:T(8,128)}, f32[256,1024]{1,0:T(8,128)}, u32[]{:S(2)}, u32[]{:S(2)}) collective-permute-start(f32[256,1024]{1,0:T(8,128)} %param.2), channel_id=1, source_target_pairs={{2,0},{3,1},{0,2},{1,3},{6,4},{7,5},{4,6},{5,7},{10,8},{11,9},{8,1... | collective-permute-start | bytes 3145736 | tf_op jit(solution)/shard_map/ppermute | solution.py:18
  5.3 96.6 %collective-permute-start.3 = (f32[256,1024]{1,0:T(8,128)}, f32[256,1024]{1,0:T(8,128)}, u32[]{:S(2)}, u32[]{:S(2)}) collective-permute-start(f32[256,1024]{1,0:T(8,128)} %param.2), channel_id=1, source_target_pairs={{1,0},{2,1},{3,2},{0,3},{5,4},{6,5},{7,6},{4,7},{9,8},{10,9},{11,1... | collective-permute-start | bytes 3145736 | tf_op jit(solution)/shard_map/ppermute | solution.py:18
  7.3 88.2 %collective-permute-start.1 = (f32[256,1024]{1,0:T(8,128)}, f32[256,1024]{1,0:T(8,128)}, u32[]{:S(2)}, u32[]{:S(2)}) collective-permute-start(f32[256,1024]{1,0:T(8,128)} %param.3), channel_id=1, source_target_pairs={{2,0},{3,1},{0,2},{1,3},{6,4},{7,5},{4,6},{5,7},{10,8},{11,9},{8,1... | collective-permute-start | bytes 3145736 | tf_op jit(solution)/shard_map/ppermute | solution.py:18
  24.9 79.2 %collective-permute-start = (f32[256,1024]{1,0:T(8,128)S(1)}, f32[256,1024]{1,0:T(8,128)S(1)}, u32[]{:S(2)}, u32[]{:S(2)}) collective-permute-start(f32[256,1024]{1,0:T(8,128)S(1)} %copy-done.2), channel_id=1, source_target_pairs={{1,0},{2,1},{3,2},{0,3},{5,4},{6,5},{7,6},{4,7},{9,8},{10,9},{11,1... | collective-permute-start | bytes 3145736 | tf_op jit(solution)/shard_map/ppermute | solution.py:18
  115.6 1.6 copy-start.5
  118.4 4.8 %collective-permute-start.6 = (f32[384,8,128]{2,1,0:T(8,128)}, f32[384,8,128]{2,1,0:T(8,128)S(1)}, u32[]{:S(2)}, u32[]{:S(2)}) collective-permute-start(f32[384,8,128]{2,1,0:T(8,128)} %constant_dynamic-slice_fusion.2), channel_id=1, source_target_pairs={{4,0},{0,4},{5,1},{1,5},{6,2},{2,6},{7,3},{3,7},{12,8},{8,12},{13,... | collective-permute-start | bytes 4718600 | tf_op jit(solution)/shard_map/ppermute | solution.py:18
  183.7 6.6 %collective-permute-start.7 = (f32[96,8,128]{2,1,0:T(8,128)S(1)}, f32[96,8,128]{2,1,0:T(8,128)S(1)}, u32[]{:S(2)}, u32[]{:S(2)}) collective-permute-start(f32[96,8,128]{2,1,0:T(8,128)S(1)} %bitcast.103), channel_id=1, source_target_pairs={{8,0},{16,8},{24,16},{0,24},{9,1},{17,9},{25,17},{1,25},{10,2},{18... | collective-permute-start | bytes 1179656 | tf_op jit(solution)/shard_map/ppermute | solution.py:18
  184.6 8.2 %collective-permute-start.8 = (f32[96,8,128]{2,1,0:T(8,128)S(1)}, f32[96,8,128]{2,1,0:T(8,128)S(1)}, u32[]{:S(2)}, u32[]{:S(2)}) collective-permute-start(f32[96,8,128]{2,1,0:T(8,128)S(1)} %bitcast.104), channel_id=1, source_target_pairs={{16,0},{24,8},{0,16},{8,24},{17,1},{25,9},{1,17},{9,25},{18,2},{26... | collective-permute-start | bytes 1179656 | tf_op jit(solution)/shard_map/ppermute | solution.py:18
  185.8 18.3 %collective-permute-start.9 = (f32[96,8,128]{2,1,0:T(8,128)S(1)}, f32[96,8,128]{2,1,0:T(8,128)S(1)}, u32[]{:S(2)}, u32[]{:S(2)}) collective-permute-start(f32[96,8,128]{2,1,0:T(8,128)S(1)} %bitcast.105), channel_id=1, source_target_pairs={{24,0},{0,8},{8,16},{16,24},{25,1},{1,9},{9,17},{17,25},{26,2},{2,... | collective-permute-start | bytes 1179656 | tf_op jit(solution)/shard_map/ppermute | solution.py:18
  204.4 37.1 %collective-permute-start.15 = (f32[384,8,128]{2,1,0:T(8,128)S(1)}, f32[384,8,128]{2,1,0:T(8,128)}, u32[]{:S(2)}, u32[]{:S(2)}) collective-permute-start(f32[384,8,128]{2,1,0:T(8,128)S(1)} %bitcast.99), channel_id=1, source_target_pairs={{3,0},{0,1},{1,2},{2,3},{7,4},{4,5},{5,6},{6,7},{11,8},{8,9},{9,10... | collective-permute-start | bytes 4718600 | tf_op jit(solution)/shard_map/ppermute | solution.py:18
  204.5 71.8 %collective-permute-start.11 = (f32[384,8,128]{2,1,0:T(8,128)S(1)}, f32[384,8,128]{2,1,0:T(8,128)}, u32[]{:S(2)}, u32[]{:S(2)}) collective-permute-start(f32[384,8,128]{2,1,0:T(8,128)S(1)} %bitcast.100), channel_id=1, source_target_pairs={{1,0},{2,1},{3,2},{0,3},{5,4},{6,5},{7,6},{4,7},{9,8},{10,9},{11,1... | collective-permute-start | bytes 4718600 | tf_op jit(solution)/shard_map/ppermute | solution.py:18
  207.1 69.2 %collective-permute-start.13 = (f32[384,8,128]{2,1,0:T(8,128)S(1)}, f32[384,8,128]{2,1,0:T(8,128)}, u32[]{:S(2)}, u32[]{:S(2)}) collective-permute-start(f32[384,8,128]{2,1,0:T(8,128)S(1)} %bitcast.101), channel_id=1, source_target_pairs={{2,0},{3,1},{0,2},{1,3},{6,4},{7,5},{4,6},{5,7},{10,8},{11,9},{8,1... | collective-permute-start | bytes 4718600 | tf_op jit(solution)/shard_map/ppermute | solution.py:18
  207.1 69.7 %collective-permute-start.10 = (f32[384,8,128]{2,1,0:T(8,128)S(1)}, f32[384,8,128]{2,1,0:T(8,128)}, u32[]{:S(2)}, u32[]{:S(2)}) collective-permute-start(f32[384,8,128]{2,1,0:T(8,128)S(1)} %bitcast.102), channel_id=1, source_target_pairs={{4,0},{0,4},{5,1},{1,5},{6,2},{2,6},{7,3},{3,7},{12,8},{8,12},{13,... | collective-permute-start | bytes 4718600 | tf_op jit(solution)/shard_map/ppermute | solution.py:18
  241.5 38.2 %collective-permute-start.16 = (f32[384,8,128]{2,1,0:T(8,128)}, f32[384,8,128]{2,1,0:T(8,128)}, u32[]{:S(2)}, u32[]{:S(2)}) collective-permute-start(f32[384,8,128]{2,1,0:T(8,128)} %collective-permute-done.15), channel_id=1, source_target_pairs={{4,0},{0,4},{5,1},{1,5},{6,2},{2,6},{7,3},{3,7},{12,8},{8,12},{13,... | collective-permute-start | bytes 4718600 | tf_op jit(solution)/shard_map/ppermute | solution.py:18
  276.3 7.9 %collective-permute-start.12 = (f32[384,8,128]{2,1,0:T(8,128)}, f32[384,8,128]{2,1,0:T(8,128)}, u32[]{:S(2)}, u32[]{:S(2)}) collective-permute-start(f32[384,8,128]{2,1,0:T(8,128)} %collective-permute-done.11), channel_id=1, source_target_pairs={{4,0},{0,4},{5,1},{1,5},{6,2},{2,6},{7,3},{3,7},{12,8},{8,12},{13,... | collective-permute-start | bytes 4718600 | tf_op jit(solution)/shard_map/ppermute | solution.py:18
  276.3 10.5 %collective-permute-start.14 = (f32[384,8,128]{2,1,0:T(8,128)}, f32[384,8,128]{2,1,0:T(8,128)S(1)}, u32[]{:S(2)}, u32[]{:S(2)}) collective-permute-start(f32[384,8,128]{2,1,0:T(8,128)} %collective-permute-done.13), channel_id=1, source_target_pairs={{4,0},{0,4},{5,1},{1,5},{6,2},{2,6},{7,3},{3,7},{12,8},{8,12},{13,... | collective-permute-start | bytes 4718600 | tf_op jit(solution)/shard_map/ppermute | solution.py:18
  278.9 19.2 %copy-start.11 = (f32[256,1024]{1,0:T(8,128)}, f32[256,1024]{1,0:T(8,128)S(1)}, u32[]{:S(2)}) copy-start(f32[256,1024]{1,0:T(8,128)S(1)} %get-tuple-element.8) | copy-start | bytes 3145732
  278.9 19.2 %copy-start.19 = (f32[256,1024]{1,0:T(8,128)}, f32[256,1024]{1,0:T(8,128)S(1)}, u32[]{:S(2)}) copy-start(f32[256,1024]{1,0:T(8,128)S(1)} %get-tuple-element.10) | copy-start | bytes 3145732
  289.2 8.9 %copy-start.6 = (f32[256,1024]{1,0:T(8,128)}, f32[256,1024]{1,0:T(8,128)S(1)}, u32[]{:S(2)}) copy-start(f32[256,1024]{1,0:T(8,128)S(1)} %get-tuple-element.13) | copy-start | bytes 3145732
  289.2 8.9 %copy-start.13 = (f32[256,1024]{1,0:T(8,128)}, f32[256,1024]{1,0:T(8,128)S(1)}, u32[]{:S(2)}) copy-start(f32[256,1024]{1,0:T(8,128)S(1)} %get-tuple-element.14) | copy-start | bytes 3145732
  289.8 8.2 %copy-start.8 = (f32[256,1024]{1,0:T(8,128)}, f32[256,1024]{1,0:T(8,128)S(1)}, u32[]{:S(2)}) copy-start(f32[256,1024]{1,0:T(8,128)S(1)} %get-tuple-element.15) | copy-start | bytes 3145732
  289.8 8.2 %copy-start.10 = (f32[256,1024]{1,0:T(8,128)}, f32[256,1024]{1,0:T(8,128)S(1)}, u32[]{:S(2)}) copy-start(f32[256,1024]{1,0:T(8,128)S(1)} %get-tuple-element.28) | copy-start | bytes 3145732
  289.8 8.2 %copy-start.15 = (f32[256,1024]{1,0:T(8,128)}, f32[256,1024]{1,0:T(8,128)S(1)}, u32[]{:S(2)}) copy-start(f32[256,1024]{1,0:T(8,128)S(1)} %get-tuple-element.16) | copy-start | bytes 3145732
  289.8 8.2 %copy-start.17 = (f32[256,1024]{1,0:T(8,128)}, f32[256,1024]{1,0:T(8,128)S(1)}, u32[]{:S(2)}) copy-start(f32[256,1024]{1,0:T(8,128)S(1)} %get-tuple-element.27) | copy-start | bytes 3145732
  290.9 7.1 %copy-start = (f32[1024,1024]{1,0:T(8,128)}, f32[1024,1024]{1,0:T(8,128)S(1)}, u32[]{:S(2)}) copy-start(f32[1024,1024]{1,0:T(8,128)S(1)} %fusion) | copy-start | bytes 12582916
  312.4 13.7 %copy-start.3 = (f32[1024,1024]{1,0:T(8,128)S(1)}, f32[1024,1024]{1,0:T(8,128)}, u32[]{:S(2)}) copy-start(f32[1024,1024]{1,0:T(8,128)} %fusion.16) | copy-start | bytes 12582916
  312.4 13.7 %copy-start.4 = (f32[1024,1024]{0,1:T(8,128)S(1)}, f32[1024,1024]{0,1:T(8,128)}, u32[]{:S(2)}) copy-start(f32[1024,1024]{0,1:T(8,128)} %copy.29) | copy-start | bytes 12582916
  339.8 5.5 %copy-start.7 = (f32[256,1024]{1,0:T(8,128)S(1)}, f32[256,1024]{1,0:T(8,128)}, u32[]{:S(2)}) copy-start(f32[256,1024]{1,0:T(8,128)} %copy-done.6) | copy-start | bytes 3145732
  339.8 5.5 %copy-start.9 = (f32[256,1024]{1,0:T(8,128)S(1)}, f32[256,1024]{1,0:T(8,128)}, u32[]{:S(2)}) copy-start(f32[256,1024]{1,0:T(8,128)} %copy-done.8) | copy-start | bytes 3145732
  345.3 5.6 %copy-start.14 = (f32[256,1024]{1,0:T(8,128)S(1)}, f32[256,1024]{1,0:T(8,128)}, u32[]{:S(2)}) copy-start(f32[256,1024]{1,0:T(8,128)} %copy-done.13) | copy-start | bytes 3145732
  345.3 5.6 %copy-start.16 = (f32[256,1024]{1,0:T(8,128)S(1)}, f32[256,1024]{1,0:T(8,128)}, u32[]{:S(2)}) copy-start(f32[256,1024]{1,0:T(8,128)} %copy-done.15) | copy-start | bytes 3145732
  345.4 5.6 %copy-start.18 = (f32[256,1024]{1,0:T(8,128)S(1)}, f32[256,1024]{1,0:T(8,128)}, u32[]{:S(2)}) copy-start(f32[256,1024]{1,0:T(8,128)} %copy-done.17) | copy-start | bytes 3145732
  345.4 5.6 %copy-start.20 = (f32[256,1024]{1,0:T(8,128)S(1)}, f32[256,1024]{1,0:T(8,128)}, u32[]{:S(2)}) copy-start(f32[256,1024]{1,0:T(8,128)} %copy-done.19) | copy-start | bytes 3145732
  350.9 2.2 copy-start.1
  359.8 4.1 %copy-start.12 = (f32[256,1024]{1,0:T(8,128)S(1)}, f32[256,1024]{1,0:T(8,128)}, u32[]{:S(2)}) copy-start(f32[256,1024]{1,0:T(8,128)} %param.2) | copy-start | bytes 3145732
